TPU v7x, 1024 devices: a whole 4x4x32 slice. The times are simulated.
1024 devices in a mesh: by: 64 (over z, core), bx: 16 (over y, x).
Axes of the slice: x: 4, y: 4, z: 32, core: 2. Of those that a mesh axis runs over, the one named last changes fastest.
Arguments:
- temp: float32 [48, 512, 2048], P(None, 'by', 'bx'), may hold values from -6 to 6
- uvel: float32 [48, 512, 2048], P(None, 'by', 'bx'), may hold values from -6 to 6
- vvel: float32 [48, 512, 2048], P(None, 'by', 'bx'), may hold values from -6 to 6
- kmt: int32 [512, 2048], P('by', 'bx'), may hold values from 0 to 48, as said below
Outputs:
- temp_new: float32 [48, 512, 2048], P(None, 'by', 'bx')
- uvel_new: float32 [48, 512, 2048], P(None, 'by', 'bx')
- vvel_new: float32 [48, 512, 2048], P(None, 'by', 'bx')
- surface: float32 [512, 2048], P('by', 'bx')
- residual: float32 [512, 2048], P('by', 'bx')
Inputs may be any that keep to these rules, and one draw needn't show every extreme that they name: kmt is 0 on land; land comes in patches of 4 x 4 cells; ocean columns have 1 to 48 active levels.
All inputs are finite; a program needn't handle non-finite values.
Results may differ from a plain program's by a relative error of at most 0.0012.
Values sent between devices are 32-bit elements; how exact they have to be, the bound alone decides.
A program may use at most 32 MiB of HBM per device.

v0:
```python
import math

import jax
import jax.numpy as jnp
from jax import lax
from jax.sharding import PartitionSpec as P

ITERS = 3


STEP_DIFF = 0.1
STEP_ADV = 0.5
STEP_SMOOTH = 0.1
STEP_VERT = 0.2
SURFACE_TERM = 0.25


def extended(value, sides, width):
    for axis, dim in sides:
        size, length = (lax.axis_size(axis), value.shape[dim])
        up = [(i, (i + 1) % size) for i in range(size)]
        down = [(j, i) for i, j in up]
        last = lax.slice_in_dim(value, length - width, length, axis=dim)
        first = lax.slice_in_dim(value, 0, width, axis=dim)
        before = lax.ppermute(last, axis, up)
        after = lax.ppermute(first, axis, down)
        value = jnp.concatenate([before, value, after], axis=dim)
    return value


def faces(padded):
    return (
        padded[..., 1:-1, 2:],
        padded[..., 1:-1, :-2],
        padded[..., 2:, 1:-1],
        padded[..., :-2, 1:-1],
    )


def centre(padded):
    return padded[..., 1:-1, 1:-1]


def level_mask(depth, levels):
    index = lax.broadcasted_iota(jnp.int32, (levels,) + depth.shape, 0).astype(jnp.float32)
    return (index < depth[None]).astype(jnp.float32)


def laplace(field_p, mask_p):
    field_c = centre(field_p)
    mask_c = centre(mask_p)
    total = jnp.zeros_like(field_c)
    for field_n, mask_n in zip(faces(field_p), faces(mask_p)):
        total = total + mask_c * mask_n * (field_n - field_c)
    return total


def section_one(field_p, mask_p):
    field_c = centre(field_p)
    east, west, north, south = faces(field_p)
    advect = 0.5 * (field_c[1] * (east - west) + field_c[2] * (north - south))
    return centre(mask_p) * (field_c + STEP_DIFF * laplace(field_p, mask_p) - STEP_ADV * advect)


def vertical(field, mask):
    zero_f = jnp.zeros_like(field[:, :1])
    zero_m = jnp.zeros_like(mask[:1])
    field_up = jnp.concatenate([field[:, 1:], zero_f], axis=1)
    field_dn = jnp.concatenate([zero_f, field[:, :-1]], axis=1)
    mask_up = jnp.concatenate([mask[1:], zero_m], axis=0)
    mask_dn = jnp.concatenate([zero_m, mask[:-1]], axis=0)
    return mask * (mask_up * (field_up - field) + mask_dn * (field_dn - field))


def section_two(star_p, mask_p):
    star_c = centre(star_p)
    mask_c = centre(mask_p)
    return mask_c * (
        star_c + STEP_SMOOTH * laplace(star_p, mask_p) + STEP_VERT * vertical(star_c, mask_c)
    )


def face_weights(depth_p, levels):
    height = depth_p / float(levels)
    height_c = centre(height)
    weights = [jnp.minimum(height_c, height_n) for height_n in faces(height)]
    diag = SURFACE_TERM + weights[0] + weights[1] + weights[2] + weights[3]
    return (weights, diag)


def apply_surface(field_p, weights, diag):
    result = diag * centre(field_p)
    for weight, field_n in zip(weights, faces(field_p)):
        result = result - weight * field_n
    return result


def zero_edges(padded, width):
    count = lax.axis_size("by")
    index = lax.axis_index("by")
    rows = lax.broadcasted_iota(jnp.int32, padded.shape, 1)
    height = padded.shape[1]
    lower = jnp.logical_and(rows < width, index == 0)
    upper = jnp.logical_and(rows >= height - width, index == count - 1)
    return jnp.where(jnp.logical_or(lower, upper), jnp.float32(0.0), padded)


def operate(direction, weights, diag):
    padded = extended(direction, (("by", 0), ("bx", 1)), 1)
    return apply_surface(padded, weights, diag)


def global_total(value):
    partial_sum = lax.psum(value, "bx")
    return lax.psum(partial_sum, "by")


def on_device(temp, uvel, vvel, kmt):
    levels, rows, cols = temp.shape
    depth = kmt.astype(jnp.float32)
    stacked = jnp.concatenate([temp, uvel, vvel, depth[None]], axis=0)
    padded = extended(stacked, (("by", 1), ("bx", 2)), 2)
    padded = zero_edges(padded, 2)
    field_p = padded[: 3 * levels].reshape(3, levels, rows + 4, cols + 4)
    depth_p = padded[3 * levels]
    mask_p = level_mask(depth_p, levels)
    star = section_one(field_p, mask_p)
    updated = section_two(star, centre(mask_p))
    depth_near = centre(depth_p)
    rhs = jnp.sum(updated[0], axis=0) / math.sqrt(levels)
    weights, diag = face_weights(depth_near, levels)
    inverse = 1.0 / diag
    solution = jnp.zeros_like(rhs)
    resid = rhs
    precond = resid * inverse
    direction = precond
    rz_now = global_total(jnp.sum(resid * precond))
    for step in range(ITERS):
        image = operate(direction, weights, diag)
        alpha = rz_now / global_total(jnp.sum(direction * image))
        solution = solution + alpha * direction
        resid = resid - alpha * image
        if step + 1 < ITERS:
            precond = resid * inverse
            rz_next = global_total(jnp.sum(resid * precond))
            direction = precond + rz_next / rz_now * direction
            rz_now = rz_next
    return (updated[0], updated[1], updated[2], solution, resid)


def solution(mesh):
    in_specs = (P(None, "by", "bx"), P(None, "by", "bx"), P(None, "by", "bx"), P("by", "bx"))
    out_specs = (
        P(None, "by", "bx"),
        P(None, "by", "bx"),
        P(None, "by", "bx"),
        P("by", "bx"),
        P("by", "bx"),
    )
    return jax.shard_map(
        on_device, mesh=mesh, in_specs=in_specs, out_specs=out_specs, check_vma=False
    )
```

profile of v0, /device:TPU:1, one launch (start us, length us, event | category | flops | bytes accessed | tf_op | source)
XLA Modules:
  0.0 763.1 jit_solution(6222512635084529009)
XLA Ops:
  0.6 0.7 convert_bitcast_fusion
  1.3 1.4 pad_maximum_fusion.4
  2.8 14.2 %collective-permute-start.1 = (f32[145,2,128]{2,1,0:T(2,128)S(1)}, f32[145,2,128]{2,1,0:T(2,128)S(1)}, u32[]{:S(2)}, u32[]{:S(2)}) collective-permute-start(f32[145,2,128]{2,1,0:T(2,128)S(1)} %get-tuple-element.40), channel_id=1, source_target_pairs={{16,0},{32,16},{48,32},{64,48},{80,64},{96,80},{112,96},{128,112},... | collective-permute-start | bytes 445448 | tf_op jit(solution)/shard_map/ppermute | solution.py:26
  16.9 1.0 collective-permute-done.1
  17.9 3.4 collective-permute-done
  21.4 1.3 pad_maximum_fusion
  23.6 6.8 collective-permute-start.3
  31.0 2.1 collective-permute-start.2
  33.1 0.8 copy.22
  33.9 5.1 collective-permute-done.2
  39.0 0.8 copy.21
  39.9 1.6 maximum_select_fusion
  41.5 1.4 copy-done
  44.2 1.1 slice-done
  45.3 1.0 copy.23
  46.6 1.6 subtract_multiply_fusion
  48.7 0.7 fusion.5
  49.6 6.4 collective-permute-start.5
  56.9 1.9 collective-permute-start.7
  58.8 6.7 collective-permute-start.6
  65.5 0.8 collective-permute-done.6
  66.2 0.7 multiply_reduce_fusion.4
  66.9 34.1 %all-reduce.5 = (f32[]{:T(128)}, f32[]{:T(128)}) all-reduce(f32[]{:T(128)} %get-tuple-element.11, f32[]{:T(128)} %get-tuple-element.10), channel_id=1, replica_groups=mesh['by'=64,'bx'=16] {'bx'}, use_global_device_ids=true, to_apply=%region_2.3 | all-reduce | flops 2 | bytes 16 | tf_op jit(solution)/shard_map/psum | solution.py:114
  101.1 102.3 %all-reduce.4 = (f32[]{:T(128)}, f32[]{:T(128)}) all-reduce(f32[]{:T(128)} %get-tuple-element.14, f32[]{:T(128)} %get-tuple-element.15), channel_id=1, replica_groups=mesh['by'=64,'bx'=16] {'by'}, use_global_device_ids=true, to_apply=%region_3.4 | all-reduce | flops 2 | bytes 16 | tf_op jit(solution)/shard_map/psum | solution.py:115
  204.8 0.6 multiply_reduce_fusion.3
  205.4 29.1 %psum.88 = f32[]{:T(128)} all-reduce(f32[]{:T(128)} %get-tuple-element.23), channel_id=1, replica_groups=mesh['by'=64,'bx'=16] {'bx'}, use_global_device_ids=true, to_apply=%region_8.9 | all-reduce | flops 1 | bytes 8 | tf_op jit(solution)/shard_map/psum | solution.py:114
  234.5 97.9 %psum.89 = f32[]{:T(128)} all-reduce(f32[]{:T(128)} %psum.88), channel_id=1, replica_groups=mesh['by'=64,'bx'=16] {'by'}, use_global_device_ids=true, to_apply=%region_9.10 | all-reduce | flops 1 | bytes 8 | tf_op jit(solution)/shard_map/psum | solution.py:115
  333.7 0.7 collective-permute-start.9
  335.0 1.7 collective-permute-done.9
  336.8 3.6 collective-permute-start.11
  340.4 5.0 collective-permute-start.10
  345.4 0.8 collective-permute-done.10
  346.2 0.7 multiply_reduce_fusion.2
  346.9 34.1 %psum.90 = f32[]{:T(128)} all-reduce(f32[]{:T(128)} %get-tuple-element.21), channel_id=1, replica_groups=mesh['by'=64,'bx'=16] {'bx'}, use_global_device_ids=true, to_apply=%region_11.12 | all-reduce | flops 1 | bytes 8 | tf_op jit(solution)/shard_map/psum | solution.py:114
  381.0 100.8 %psum.91 = f32[]{:T(128)} all-reduce(f32[]{:T(128)} %psum.90), channel_id=1, replica_groups=mesh['by'=64,'bx'=16] {'by'}, use_global_device_ids=true, to_apply=%region_12.13 | all-reduce | flops 1 | bytes 8 | tf_op jit(solution)/shard_map/psum | solution.py:115
  483.8 29.1 %psum.92 = f32[]{:T(128)} all-reduce(f32[]{:T(128)} %get-tuple-element.18), channel_id=1, replica_groups=mesh['by'=64,'bx'=16] {'bx'}, use_global_device_ids=true, to_apply=%region_14.15 | all-reduce | flops 1 | bytes 8 | tf_op jit(solution)/shard_map/psum | solution.py:114
  512.9 97.9 %psum.93 = f32[]{:T(128)} all-reduce(f32[]{:T(128)} %psum.92), channel_id=1, replica_groups=mesh['by'=64,'bx'=16] {'by'}, use_global_device_ids=true, to_apply=%region_15.16 | all-reduce | flops 1 | bytes 8 | tf_op jit(solution)/shard_map/psum | solution.py:115
  612.2 0.7 collective-permute-start.13
  612.8 0.7 copy.24
  613.6 0.7 copy.25
  614.3 0.8 collective-permute-done.13
  615.2 3.6 collective-permute-start.15
  618.9 5.0 collective-permute-start.14
  623.8 0.8 collective-permute-done.14
  624.6 0.7 multiply_reduce_fusion
  625.3 34.3 %psum.94 = f32[]{:T(128)} all-reduce(f32[]{:T(128)} %get-tuple-element.16), channel_id=1, replica_groups=mesh['by'=64,'bx'=16] {'bx'}, use_global_device_ids=true, to_apply=%region_17.18 | all-reduce | flops 1 | bytes 8 | tf_op jit(solution)/shard_map/psum | solution.py:114
  659.5 0.7 copy.26
  660.3 100.9 %psum.95 = f32[]{:T(128)} all-reduce(f32[]{:T(128)} %psum.94), channel_id=1, replica_groups=mesh['by'=64,'bx'=16] {'by'}, use_global_device_ids=true, to_apply=%region_18.19 | all-reduce | flops 1 | bytes 8 | tf_op jit(solution)/shard_map/psum | solution.py:115
  (50 shorter events, 6.5 us)
Async XLA Ops:
  2.8 15.2 %collective-permute-start.1 = (f32[145,2,128]{2,1,0:T(2,128)S(1)}, f32[145,2,128]{2,1,0:T(2,128)S(1)}, u32[]{:S(2)}, u32[]{:S(2)}) collective-permute-start(f32[145,2,128]{2,1,0:T(2,128)S(1)} %get-tuple-element.40), channel_id=1, source_target_pairs={{16,0},{32,16},{48,32},{64,48},{80,64},{96,80},{112,96},{128,112},... | collective-permute-start | bytes 445448 | tf_op jit(solution)/shard_map/ppermute | solution.py:26
  16.9 4.4 collective-permute-start
  23.6 9.5 %collective-permute-start.3 = (f32[145,12,2]{0,2,1:T(2,128)S(1)}, f32[145,12,2]{0,2,1:T(2,128)S(1)}, u32[]{:S(2)}, u32[]{:S(2)}) collective-permute-start(f32[145,12,2]{0,2,1:T(2,128)S(1)} %copy.20), channel_id=1, source_target_pairs={{1,0},{2,1},{3,2},{4,3},{5,4},{6,5},{7,6},{8,7},{9,8},{10,9},{11,1... | collective-permute-start | bytes 41768 | tf_op jit(solution)/shard_map/ppermute | solution.py:26
  31.0 8.9 %copy-start.1 = (f32[48,8,128]{2,1,0:T(8,128)S(1)}, f32[48,8,128]{2,1,0:T(8,128)}, u32[]{:S(2)}) copy-start(f32[48,8,128]{2,1,0:T(8,128)} %param.6) | copy-start | bytes 589828
  31.0 8.9 %copy-start.2 = (f32[48,8,128]{2,1,0:T(8,128)S(1)}, f32[48,8,128]{2,1,0:T(8,128)}, u32[]{:S(2)}) copy-start(f32[48,8,128]{2,1,0:T(8,128)} %param.5) | copy-start | bytes 589828
  31.0 8.9 %copy-start.3 = (f32[48,8,128]{2,1,0:T(8,128)S(1)}, f32[48,8,128]{2,1,0:T(8,128)}, u32[]{:S(2)}) copy-start(f32[48,8,128]{2,1,0:T(8,128)} %param.4) | copy-start | bytes 589828
  31.0 8.0 %collective-permute-start.2 = (f32[145,12,2]{0,2,1:T(2,128)S(1)}, f32[145,12,2]{0,2,1:T(2,128)S(1)}, u32[]{:S(2)}, u32[]{:S(2)}) collective-permute-start(f32[145,12,2]{0,2,1:T(2,128)S(1)} %copy.19), channel_id=1, source_target_pairs={{0,1},{1,2},{2,3},{3,4},{4,5},{5,6},{6,7},{7,8},{8,9},{9,10},{10,1... | collective-permute-start | bytes 41768 | tf_op jit(solution)/shard_map/ppermute | solution.py:25
  41.5 1.4 copy-start
  43.6 1.7 slice-start
  49.6 7.0 collective-permute-start.4
  49.6 7.2 collective-permute-start.5
  56.9 8.6 %collective-permute-start.7 = (f32[10,1]{1,0:T(8,128)S(1)}, f32[10,1]{1,0:T(8,128)S(1)}, u32[]{:S(2)}, u32[]{:S(2)}) collective-permute-start(f32[10,1]{1,0:T(8,128)S(1)} %get-tuple-element.62), channel_id=1, source_target_pairs={{0,1},{1,2},{2,3},{3,4},{4,5},{5,6},{6,7},{7,8},{8,9},{9,10},{10,1... | collective-permute-start | bytes 128 | tf_op jit(solution)/shard_map/ppermute | solution.py:25
  58.8 7.5 collective-permute-start.6
  333.7 1.3 collective-permute-start.8
  333.7 3.0 collective-permute-start.9
  336.8 8.6 %collective-permute-start.11 = (f32[10,1]{1,0:T(8,128)S(1)}, f32[10,1]{1,0:T(8,128)S(1)}, u32[]{:S(2)}, u32[]{:S(2)}) collective-permute-start(f32[10,1]{1,0:T(8,128)S(1)} %get-tuple-element.60), channel_id=1, source_target_pairs={{0,1},{1,2},{2,3},{3,4},{4,5},{5,6},{6,7},{7,8},{8,9},{9,10},{10,1... | collective-permute-start | bytes 128 | tf_op jit(solution)/shard_map/ppermute | solution.py:25
  340.4 5.7 collective-permute-start.10
  612.1 2.2 collective-permute-start.12
  612.2 3.0 collective-permute-start.13
  615.2 8.6 %collective-permute-start.15 = (f32[10,1]{1,0:T(8,128)S(1)}, f32[10,1]{1,0:T(8,128)S(1)}, u32[]{:S(2)}, u32[]{:S(2)}) collective-permute-start(f32[10,1]{1,0:T(8,128)S(1)} %get-tuple-element.58), channel_id=1, source_target_pairs={{0,1},{1,2},{2,3},{3,4},{4,5},{5,6},{6,7},{7,8},{8,9},{9,10},{10,1... | collective-permute-start | bytes 128 | tf_op jit(solution)/shard_map/ppermute | solution.py:25
  618.9 5.7 collective-permute-start.14
where the time goes:
time: 764 us; the launch traced here: 763 us
  blocking collectives  661 us (87%)
  starting transfers between devices  56.6 us (7%)
  waiting for transfers between devices  15.8 us (2%)
  other arithmetic  12.5 us (2%)
  local copies, waits for them, and re-layouts  9.96 us (1%)
  between operations  7.66 us (1%)
    psum x5, blocking collectives, global_total(): return lax.psum(partial_sum, 'by')  500 us
    psum x5, blocking collectives, global_total(): partial_sum = lax.psum(value, 'bx')  161 us
    ppermute x8, starting transfers between devices, extended(): after = lax.ppermute(first, axis, down)  45.3 us
  transfers between devices with their start and end apart: 16, of which 11 were waited for; matrix products, arithmetic and copies ran while one was open for 0% of the time, Pallas kernels for 0%

commit v1 on v0

v1 whole, which is shorter than its diff:
```python
import math

import jax
import jax.numpy as jnp
from jax import lax
from jax.experimental import pallas as pl
from jax.experimental.pallas import tpu as pltpu
from jax.sharding import PartitionSpec as P

ITERS = 3
STEP_DIFF = 0.1
STEP_ADV = 0.5
STEP_SMOOTH = 0.1
STEP_VERT = 0.2
SURFACE_TERM = 0.25

KL, ROWS, COLS = 48, 8, 128
CHUNK = 8
PITCH = 16
PADDED = PITCH * (KL + 2)
RADIUS = 4

F32 = jnp.float32
MESH = pl.DeviceIdType.MESH

DIRS = [(-1, -1), (-1, 0), (-1, 1), (0, -1), (0, 1), (1, -1), (1, 0), (1, 1)]
SW, S, SE, W, E, NW, N, NE = range(8)

GRAM = [(i, j) for i in range(ITERS + 1) for j in range(i, ITERS + 1)]


def roll(value, shift, axis):
    size = value.shape[axis]
    return pltpu.roll(value, shift % size if isinstance(shift, int) else shift, axis)


def lanes_of(shape):
    return lax.broadcasted_iota(jnp.int32, shape, len(shape) - 1)


def east_west(value, edge):
    lane = lanes_of(value.shape)
    axis = value.ndim - 1
    east = roll(jnp.where(lane == 0, edge, value), -1, axis)
    west = roll(jnp.where(lane == COLS - 1, edge, value), 1, axis)
    return east, west


def star_terms(level, depths, uvel, vvel):
    centre = level < depths[0]
    diff = [jnp.where(level < d, F32(STEP_DIFF), F32(0.0)) for d in depths[1:]]
    own = F32(1.0) - ((diff[0] + diff[1]) + (diff[2] + diff[3]))
    adv_u = F32(0.5 * STEP_ADV) * uvel
    adv_v = F32(0.5 * STEP_ADV) * vvel
    return centre, own, (diff[0] - adv_u, diff[1] + adv_u, diff[2] - adv_v, diff[3] + adv_v)


def star_value(terms, cell, sides):
    centre, own, factors = terms
    total = own * cell
    for factor, side in zip(factors, sides):
        total = total + factor * side
    return jnp.where(centre, total, F32(0.0))


def kernel(
    nby, nbx,
    temp_in, uvel_in, vvel_in, kmt_in,
    temp_out, uvel_out, vvel_out, surface_out, resid_out,
    raw, kmt_v, pad_t, pad_u, pad_v, star_t, star_u, star_v, fresh, surf_v, resid_v, depth_v, depths_v, q_ref, qs_ref,
    tx_row1, tx_row2, tx_col, tx_cor, rx_row1, rx_row2, rx_col, rx_cor,
    tx_u, rx_u, tx_bx, rx_bx, tx_by, rx_by,
    in_sem, out_sem, row1_s, row1_r, row2_s, row2_r, col_s, col_r, cor_s, cor_r, u_s, u_r, bx_s, bx_r, by_s, by_r,
    known,
):
    by, bx = lax.axis_index("by"), lax.axis_index("bx")
    pads = (pad_t, pad_u, pad_v)
    stars = (star_t, star_u, star_v)

    def device(dy, dx):
        return (lax.rem(by + dy + nby, nby), lax.rem(bx + dx + nbx, nbx))

    loads = [
        pltpu.make_async_copy(src, dst, in_sem.at[i])
        for i, (src, dst) in enumerate(
            [(kmt_in, kmt_v), (temp_in, raw.at[0]), (uvel_in, raw.at[1]), (vvel_in, raw.at[2])]
        )
    ]
    for load in loads:
        load.start()

    barrier = pltpu.get_barrier_semaphore()
    greeted = [device(0, o) for o in range(1, nbx)]
    greeted += [device(d, 0) for d in range(-RADIUS, RADIUS + 1) if d]
    greeted += [device(dy, dx) for dy, dx in DIRS if dy and dx]
    for dev in greeted:
        pl.semaphore_signal(barrier, inc=1, device_id=dev, device_id_type=MESH)

    keep_s = jnp.where(by == 0, F32(0.0), F32(1.0))
    keep_n = jnp.where(by == nby - 1, F32(0.0), F32(1.0))
    lane8 = lanes_of((8, COLS))
    sub8 = lax.broadcasted_iota(jnp.int32, (8, COLS), 0)

    loads[0].wait()
    depth_v[...] = kmt_v[...].astype(F32)
    for f in range(3):
        loads[1 + f].wait()
        pad = pads[f]

        def pack(c, carry, f=f, pad=pad):
            packed = jnp.zeros((8, COLS), F32)
            rows = pad.at[pl.ds(pl.multiple_of(c * (PITCH * CHUNK), PITCH * CHUNK), PITCH * (CHUNK + 2)), :]
            for l in range(CHUNK):
                tile = raw[f, c * CHUNK + l]
                rows[pl.ds(PITCH * (l + 1), 8), :] = tile
                packed = jnp.where(lane8 // 4 == l, roll(tile, 2 + 4 * l, 1), packed)
            quarter = lax.rem(c, 4)
            packed = roll(packed, 32 * quarter, 1)
            half = c // 4
            before = tx_col[2 * f + half]
            tx_col[2 * f + half] = jnp.where(lane8 // 32 == quarter, packed, before)
            return carry

        for half in range(2):
            tx_col[2 * f + half] = jnp.zeros((8, COLS), F32)
        lax.fori_loop(0, KL // CHUNK, pack, 0)
    tx_col[6] = depth_v[...]

    def edge_row(f, row):
        return pads[f][pl.ds(PITCH + row, KL, stride=PITCH), :]

    lane_row = lanes_of((8, COLS))
    for side, (row, inner) in enumerate([(0, 1), (ROWS - 1, ROWS - 2)]):
        edges = [edge_row(f, row) for f in range(3)]
        tx_row1[side, 0:KL] = edges[0]
        tx_row1[side, KL : 2 * KL] = edge_row(0, inner)
        tx_row1[side, 2 * KL : 3 * KL] = edges[1]
        tx_row1[side, 3 * KL : 4 * KL] = edges[2]
        tx_row1[side, 4 * KL : 4 * KL + 8] = depth_v[...]
        tx_row2[side, 0:KL] = edge_row(1, inner)
        tx_row2[side, KL : 2 * KL] = edge_row(2, inner)
        corner = jnp.zeros((8, COLS), F32)
        for f in range(3):
            for g in range(6):
                at = 2 * (6 * f + g)
                corner = jnp.where(lane_row // 2 == at // 2, roll(edges[f][8 * g : 8 * g + 8], 1 + at, 1), corner)
        tx_cor[side, 0:8] = depth_v[...]
        tx_cor[side, 8:16] = corner
        for i in range(6):
            tx_cor[side, 16 + i : 17 + i] = tx_col[i, row : row + 1]
        tx_cor[side, 22:24] = jnp.zeros((2, COLS), F32)

    def remote(src, dst, send, recv, dev):
        return pltpu.make_async_remote_copy(
            src_ref=src, dst_ref=dst, send_sem=send, recv_sem=recv, device_id=dev, device_id_type=MESH
        )

    pl.semaphore_wait(barrier, len(greeted))

    south, north, west, east = device(-1, 0), device(1, 0), device(0, -1), device(0, 1)
    row1 = [
        remote(tx_row1.at[0], rx_row1.at[1], row1_s.at[0], row1_r.at[1], south),
        remote(tx_row1.at[1], rx_row1.at[0], row1_s.at[1], row1_r.at[0], north),
    ]
    cols = [
        remote(tx_col, rx_col.at[1], col_s.at[0], col_r.at[1], west),
        remote(tx_col, rx_col.at[0], col_s.at[1], col_r.at[0], east),
    ]
    diagonal = [SW, SE, NW, NE]
    cors = []
    for i, d in enumerate(diagonal):
        dy, dx = DIRS[d]
        cors.append(
            remote(tx_cor.at[0 if dy < 0 else 1], rx_cor.at[3 - i], cor_s.at[i], cor_r.at[3 - i], device(dy, dx))
        )
    row2 = [
        remote(tx_row2.at[0], rx_row2.at[1], row2_s.at[0], row2_r.at[1], south),
        remote(tx_row2.at[1], rx_row2.at[0], row2_s.at[1], row2_r.at[0], north),
    ]
    first = row1 + cols + cors
    for copy in first + row2:
        copy.start()

    def tell(step, reach):
        for d in (-reach, reach):
            pl.semaphore_signal(known.at[step], inc=1, device_id=device(d, 0), device_id_type=MESH)

    tell(0, RADIUS)

    for star in stars:
        star[0:PITCH, :] = jnp.zeros((PITCH, COLS), F32)
        star[PADDED - PITCH : PADDED, :] = jnp.zeros((PITCH, COLS), F32)

    for copy in first:
        copy.wait_recv()
    pl.semaphore_wait(known.at[0], 2)
    tell(1, 2 * RADIUS)

    dep = {
        S: keep_s * rx_row1[0, 4 * KL : 4 * KL + 8],
        N: keep_n * rx_row1[1, 4 * KL : 4 * KL + 8],
        W: rx_col[0, 6],
        E: rx_col[1, 6],
        SW: keep_s * rx_cor[0, 0:8],
        SE: keep_s * rx_cor[1, 0:8],
        NW: keep_n * rx_cor[2, 0:8],
        NE: keep_n * rx_cor[3, 0:8],
    }

    def patch(own, near):
        beside = jnp.where(lane8 < 64, near[E], near[W])
        below = jnp.where(sub8 < 4, near[N], near[S])
        across = jnp.where(
            sub8 < 4, jnp.where(lane8 < 64, near[NE], near[NW]), jnp.where(lane8 < 64, near[SE], near[SW])
        )
        return jnp.concatenate(
            [jnp.concatenate([own, beside], axis=1), jnp.concatenate([below, across], axis=1)], axis=0
        )

    depth = patch(depth_v[...], dep)
    depths = (depth, roll(depth, -1, 1), roll(depth, 1, 1), roll(depth, -1, 0), roll(depth, 1, 0))
    for i, d in enumerate(depths):
        depths_v[i] = d

    rows1 = {}
    for side, (keep, place) in enumerate([(keep_s, PITCH - 1), (keep_n, PITCH + ROWS)]):
        for f, at in ((0, 0), (1, 2), (2, 3)):
            value = keep * rx_row1[side, at * KL : (at + 1) * KL]
            pads[f][pl.ds(place, KL, stride=PITCH), :] = value
            rows1[side, f] = value

    odd = lane8 % 4 >= 2
    for i in range(6):
        q_ref[i] = jnp.where(odd, rx_col[1, i], rx_col[0, i])
    lane_corner = [
        keep * jnp.where(odd, rx_cor[2 * side + 1, 16:24], rx_cor[2 * side, 16:24])
        for side, keep in enumerate((keep_s, keep_n))
    ]
    level_corner = [
        keep * jnp.where(lane8 % 2 == 1, rx_cor[2 * side + 1, 8:16], rx_cor[2 * side, 8:16])
        for side, keep in enumerate((keep_s, keep_n))
    ]

    level_rows = lax.broadcasted_iota(jnp.int32, (KL, COLS), 0).astype(F32)

    def star_rows(fields, second):
        for side, (row, place) in enumerate([(2 * ROWS - 1, PITCH - 1), (ROWS, PITCH + ROWS)]):
            near = [depths_v[i, row : row + 1, 0:COLS] for i in range(5)]
            terms = star_terms(level_rows, near, rows1[side, 1], rows1[side, 2])
            for f in fields:
                cell = rows1[side, f]
                inner = edge_row(f, 0 if side == 0 else ROWS - 1)
                outer = second(side, f)
                edge = jnp.concatenate(
                    [roll(level_corner[side], COLS - 1 - 2 * (6 * f + g), 1) for g in range(6)], axis=0
                )
                e, w = east_west(cell, edge)
                n, s = (inner, outer) if side == 0 else (outer, inner)
                stars[f][pl.ds(place, KL, stride=PITCH), :] = star_value(terms, cell, (e, w, n, s))

    def star_cols(fields):
        near = [
            jnp.where(odd, depths_v[i, 0:8, COLS : COLS + 1], depths_v[i, 0:8, 2 * COLS - 1 : 2 * COLS]) for i in range(5)
        ]
        for half in range(2):
            level = (lane8 // 4 + 32 * half).astype(F32)
            terms = star_terms(level, near, q_ref[2 + half], q_ref[4 + half])
            for f in fields:
                i = 2 * f + half
                cell, own = q_ref[i], tx_col[i]
                e = jnp.where(odd, roll(cell, -1, 1), roll(own, -1, 1))
                w = jnp.where(odd, roll(own, 1, 1), roll(cell, 1, 1))
                n = jnp.where(sub8 == ROWS - 1, lane_corner[1][i : i + 1], roll(cell, -1, 0))
                s = jnp.where(sub8 == 0, lane_corner[0][i : i + 1], roll(cell, 1, 0))
                qs_ref[i] = star_value(terms, cell, (e, w, n, s))

    def near_own():
        return [depths_v[i, 0:8, 0:COLS] for i in range(5)]

    def chunk_rows(ref, c):
        return ref.at[pl.ds(pl.multiple_of(c * (PITCH * CHUNK), PITCH * CHUNK), PITCH * (CHUNK + 2)), :]

    def edge_of(ref, f, c, l):
        shift = lax.rem(2 * COLS - 2 - 32 * lax.rem(c, 4) - 4 * l, COLS)
        return roll(ref[2 * f + c // 4], shift, 1)

    def star_own(fields):
        def step(c, carry):
            near = near_own()
            views = [chunk_rows(pad, c) for pad in pads]
            outs = [chunk_rows(star, c) for star in stars]
            for l in range(CHUNK):
                base = PITCH * (l + 1)
                level = (c * CHUNK + l).astype(F32)
                terms = star_terms(
                    level, near, views[1][pl.ds(base, 8), :], views[2][pl.ds(base, 8), :]
                )
                for f in fields:
                    cell = views[f][pl.ds(base, 8), :]
                    e, w = east_west(cell, edge_of(q_ref, f, c, l))
                    n = views[f][pl.ds(base + 1, 8), :]
                    s = views[f][pl.ds(base - 1, 8), :]
                    outs[f][pl.ds(base, 8), :] = star_value(terms, cell, (e, w, n, s))
            return carry

        lax.fori_loop(0, KL // CHUNK, step, 0)

    def update_own(fields):
        def step(c, total):
            near = near_own()
            views = [chunk_rows(star, c) for star in stars]
            for l in range(CHUNK):
                base = PITCH * (l + 1)
                level = (c * CHUNK + l).astype(F32)
                smooth = [jnp.where(level < d, F32(STEP_SMOOTH), F32(0.0)) for d in near[1:]]
                up = jnp.where(level + F32(1.0) < near[0], F32(STEP_VERT), F32(0.0))
                down = jnp.where(level > F32(0.0), F32(STEP_VERT), F32(0.0))
                own = F32(1.0) - (((smooth[0] + smooth[1]) + (smooth[2] + smooth[3])) + (up + down))
                centre = level < near[0]
                for f in fields:
                    view = views[f]
                    cell = view[pl.ds(base, 8), :]
                    e, w = east_west(cell, edge_of(qs_ref, f, c, l))
                    n = view[pl.ds(base + 1, 8), :]
                    s = view[pl.ds(base - 1, 8), :]
                    above = view[pl.ds(base + PITCH, 8), :]
                    below = view[pl.ds(base - PITCH, 8), :]
                    value = own * cell + F32(STEP_SMOOTH) * ((e + w) + (n + s)) + F32(STEP_VERT) * (above + below)
                    value = jnp.where(centre, value, F32(0.0))
                    fresh[f, c * CHUNK + l] = value
                    if f == 0:
                        total = total + value
            return total

        return lax.fori_loop(0, KL // CHUNK, step, jnp.zeros((8, COLS), F32))

    star_rows([0], lambda side, f: (keep_s, keep_n)[side] * rx_row1[side, KL : 2 * KL])
    star_cols([0])
    star_own([0])
    rhs = update_own([0]) * F32(1.0 / math.sqrt(KL))

    height = depths_v[0] * F32(1.0 / KL)
    w_e = jnp.minimum(height, roll(height, -1, 1))
    w_n = jnp.minimum(height, roll(height, -1, 0))
    w_w = roll(w_e, 1, 1)
    w_s = roll(w_n, 1, 0)
    diag = F32(SURFACE_TERM) + w_e + w_w + w_n + w_s
    inverse = F32(1.0) / diag
    scaled = (w_e * inverse, w_w * inverse, w_n * inverse, w_s * inverse)

    tx_u[...] = rhs * inverse[0:8, 0:COLS]
    round_u = [
        remote(tx_u, rx_u.at[7 - i], u_s.at[i], u_r.at[7 - i], device(dy, dx)) for i, (dy, dx) in enumerate(DIRS)
    ]
    for copy in round_u:
        copy.start()
    saves = [
        pltpu.make_async_copy(fresh.at[f], dst, out_sem.at[f]) for f, dst in enumerate((temp_out, uvel_out, vvel_out))
    ]
    saves[0].start()
    for copy in round_u:
        copy.wait_recv()
    pl.semaphore_wait(known.at[1], 2)
    tell(2, 4 * RADIUS)

    power = patch(tx_u[...], {d: rx_u[d] for d in range(8)})
    powers = [power]
    for _ in range(ITERS):
        e, w = roll(power, -1, 1), roll(power, 1, 1)
        n, s = roll(power, -1, 0), roll(power, 1, 0)
        power = (scaled[0] * e + scaled[1] * w) + (scaled[2] * n + scaled[3] * s)
        powers.append(power)
    own_diag = diag[0:8, 0:COLS]
    powers = [p[0:8, 0:COLS] for p in powers]
    weighted = [own_diag * p for p in powers]

    row = jnp.zeros((1, COLS), F32)
    lane1 = lanes_of((1, COLS))
    for k, (i, j) in enumerate(GRAM):
        part = jnp.sum(jnp.sum(weighted[i] * powers[j], axis=0, keepdims=True), axis=1, keepdims=True)
        row = jnp.where(lane1 == k, part, row)

    tx_bx[...] = row
    over_bx = [
        remote(tx_bx, rx_bx.at[o - 1], bx_s, bx_r, device(0, o)) for o in range(1, nbx)
    ]
    for copy in over_bx:
        copy.start()
    remote(rx_bx, rx_bx, bx_s, bx_r, east).wait_recv()
    row = row + jnp.sum(rx_bx[...], axis=0)
    pl.semaphore_wait(known.at[2], 2)

    tx_by[...] = row
    order = sorted(range(1, nby), key=lambda o: -min(o, nby - o))
    over_by = [remote(tx_by, rx_by.at[o - 1], by_s, by_r, device(o, 0)) for o in order]
    for copy in over_by:
        copy.start()

    for copy in row2:
        copy.wait_recv()
    star_rows([1, 2], lambda side, f: (keep_s, keep_n)[side] * rx_row2[side, (f - 1) * KL : f * KL])
    star_cols([1, 2])
    star_own([1, 2])
    update_own([1, 2])
    saves[1].start()
    saves[2].start()
    for copy in first + row2 + round_u:
        copy.wait_send()
    remote(rx_bx, rx_bx, bx_s, bx_r, east).wait_send()

    remote(rx_by, rx_by, by_s, by_r, north).wait_recv()
    row = row + jnp.sum(rx_by[...], axis=0)

    gram = {}
    for k, (i, j) in enumerate(GRAM):
        gram[i, j] = gram[j, i] = row[0:1, k : k + 1]

    def inner(a, b):
        total = None
        for i, ai in enumerate(a):
            for j, bj in enumerate(b):
                term = ai * bj * gram[i, j]
                total = term if total is None else total + term
        return total

    one = jnp.ones((1, 1), F32)
    z, p, x = [one], [one], []
    rz = inner(z, z)
    for step in range(ITERS):
        q = [p[0]] + [p[i] - p[i - 1] for i in range(1, len(p))] + [-p[-1]]
        alpha = rz / inner(p, q)
        x = [x[i] + alpha * p[i] if i < len(x) else alpha * p[i] for i in range(len(p))]
        z = [z[i] - alpha * q[i] if i < len(z) else -(alpha * q[i]) for i in range(len(q))]
        if step + 1 < ITERS:
            rz_next = inner(z, z)
            beta = rz_next / rz
            p = [z[i] + beta * p[i] if i < len(p) else z[i] for i in range(len(z))]
            rz = rz_next

    surface = x[0] * powers[0]
    for i in range(1, ITERS):
        surface = surface + x[i] * powers[i]
    resid = z[0] * weighted[0]
    for i in range(1, ITERS + 1):
        resid = resid + z[i] * weighted[i]
    surf_v[...] = surface
    resid_v[...] = resid
    saves.append(pltpu.make_async_copy(surf_v, surface_out, out_sem.at[3]))
    saves.append(pltpu.make_async_copy(resid_v, resid_out, out_sem.at[4]))
    saves[3].start()
    saves[4].start()
    remote(rx_by, rx_by, by_s, by_r, north).wait_send()
    for save in saves:
        save.wait()


def solution(mesh):
    nby, nbx = mesh.shape["by"], mesh.shape["bx"]

    def on_device(temp, uvel, vvel, kmt):
        field = jax.ShapeDtypeStruct(temp.shape, F32)
        plane = jax.ShapeDtypeStruct(kmt.shape, F32)
        vmem, dma = pltpu.VMEM, pltpu.SemaphoreType.DMA
        return pl.pallas_call(
            lambda *refs: kernel(nby, nbx, *refs),
            out_shape=(field, field, field, plane, plane),
            in_specs=[pl.BlockSpec(memory_space=pl.ANY)] * 4,
            out_specs=(pl.BlockSpec(memory_space=pl.ANY),) * 5,
            scratch_shapes=[
                vmem((3, KL, ROWS, COLS), F32),
                vmem((ROWS, COLS), jnp.int32),
                *[vmem((PADDED, COLS), F32)] * 6,
                vmem((3, KL, ROWS, COLS), F32),
                vmem((ROWS, COLS), F32),
                vmem((ROWS, COLS), F32),
                vmem((ROWS, COLS), F32),
                vmem((5, 2 * ROWS, 2 * COLS), F32),
                vmem((6, ROWS, COLS), F32),
                vmem((6, ROWS, COLS), F32),
                vmem((2, 4 * KL + 8, COLS), F32),
                vmem((2, 2 * KL, COLS), F32),
                vmem((7, ROWS, COLS), F32),
                vmem((2, 24, COLS), F32),
                vmem((2, 4 * KL + 8, COLS), F32),
                vmem((2, 2 * KL, COLS), F32),
                vmem((2, 7, ROWS, COLS), F32),
                vmem((4, 24, COLS), F32),
                vmem((ROWS, COLS), F32),
                vmem((8, ROWS, COLS), F32),
                vmem((1, COLS), F32),
                vmem((nbx - 1, 1, COLS), F32),
                vmem((1, COLS), F32),
                vmem((nby - 1, 1, COLS), F32),
                dma((4,)), dma((5,)),
                dma((2,)), dma((2,)), dma((2,)), dma((2,)),
                dma((2,)), dma((2,)), dma((4,)), dma((4,)),
                dma((8,)), dma((8,)),
                dma, dma, dma, dma,
                pltpu.SemaphoreType.REGULAR((3,)),
            ],
            compiler_params=pltpu.CompilerParams(
                collective_id=0, has_side_effects=True, vmem_limit_bytes=32 * 1024 * 1024
            ),
        )(temp, uvel, vvel, kmt)

    in_specs = (P(None, "by", "bx"), P(None, "by", "bx"), P(None, "by", "bx"), P("by", "bx"))
    out_specs = (
        P(None, "by", "bx"),
        P(None, "by", "bx"),
        P(None, "by", "bx"),
        P("by", "bx"),
        P("by", "bx"),
    )
    return jax.shard_map(on_device, mesh=mesh, in_specs=in_specs, out_specs=out_specs, check_vma=False)
```

time: 764 us -> 63.5 us (0.08)
  blocking collectives: 661 us -> 0 us
  starting transfers between devices: 56.6 us -> 0 us
  Pallas kernels: 0 us -> 55.9 us
  waiting for transfers between devices: 15.8 us -> 0 us
  other arithmetic: 12.5 us -> 0 us
    psum x10 -> x0, blocking collectives: 661 us -> none  [the longest x5 500 us: global_total(): return lax.psum(partial_sum, 'by')]
    ppermute x16 -> x0, starting transfers between devices: 56.6 us -> none  [the longest x8 45.3 us: extended(): after = lax.ppermute(first, axis, down)]
    pallas_call x0 -> x1, Pallas kernels: none -> 55.9 us  [on_device(): pl.pallas_call(lambda *refs: kernel(nby, nbx, *refs), out_shape=(field, f...]
    ppermute x16 -> x0, waiting for transfers between devices: 15.8 us -> none  [the longest x8 9.71 us: extended(): before = lax.ppermute(last, axis, up)]
  transfers between devices with their start and end apart: 16 -> 0, of which waited for: 11 -> 0; matrix products, arithmetic and copies ran while one was open for 0% -> 0% of each run, Pallas kernels for 0% -> 0%
where the time goes in v1:
time: 63.5 us; the launch traced here: 63.2 us
  Pallas kernels  55.9 us (88%)
  local copies, waits for them, and re-layouts  6.68 us (11%)
  between operations  0.65 us (1%)
    pallas_call x1, Pallas kernels, on_device(): pl.pallas_call(lambda *refs: kernel(nby, nbx, *refs), out_shape=(field, f...  55.9 us
    unnamed x13, local copies, waits for them, and re-layouts  6.68 us

profile of v1, /device:TPU:1, one launch (start us, length us, event | category | flops | bytes accessed | tf_op | source)
XLA Modules:
  0.0 63.2 jit_solution(13823060301817601206)
XLA Ops:
  0.6 0.0 copy-start
  0.6 0.9 %copy-done = f32[48,8,128]{2,1,0:T(8,128)S(1)} copy-done((f32[48,8,128]{2,1,0:T(8,128)S(1)}, f32[48,8,128]{2,1,0:T(8,128)}, u32[]{:S(2)}) %copy-start) | copy-done | bytes 196632
  1.6 0.0 copy-start.1
  1.6 0.9 %copy-done.1 = f32[48,8,128]{2,1,0:T(8,128)S(1)} copy-done((f32[48,8,128]{2,1,0:T(8,128)S(1)}, f32[48,8,128]{2,1,0:T(8,128)}, u32[]{:S(2)}) %copy-start.1) | copy-done | bytes 196632
  2.5 0.0 copy-start.2
  2.5 0.9 %copy-done.2 = f32[48,8,128]{2,1,0:T(8,128)S(1)} copy-done((f32[48,8,128]{2,1,0:T(8,128)S(1)}, f32[48,8,128]{2,1,0:T(8,128)}, u32[]{:S(2)}) %copy-start.2) | copy-done | bytes 196632
  3.4 0.0 copy-start.3
  3.4 0.7 %copy-done.3 = s32[8,128]{1,0:T(8,128)S(1)} copy-done((s32[8,128]{1,0:T(8,128)S(1)}, s32[8,128]{1,0:T(8,128)}, u32[]{:S(2)}) %copy-start.3) | copy-done | bytes 4120
  4.1 55.9 %shard_map.83 = (f32[48,8,128]{2,1,0:T(8,128)S(1)}, f32[48,8,128]{2,1,0:T(8,128)S(1)}, f32[48,8,128]{2,1,0:T(8,128)S(1)}, f32[8,128]{1,0:T(8,128)S(1)}, f32[8,128]{1,0:T(8,128)S(1)}) custom-call(f32[48,8,128]{2,1,0:T(8,128)S(1)} %copy-done, f32[48,8,128]{2,1,0:T(8,128)S(1)} %copy-done.1, f32[48,8,128]{2,1,0:T(8,128)S(1)} %copy-done.2, s32[8,128]{1,0:T(8,128)S(1)} %copy-done.3), custom_call_target="tpu_custom_call" | custom-call | tf_op jit(solution)/shard_map/pallas_call | solution.py:464
  60.0 0.7 %copy.14 = f32[48,8,128]{2,1,0:T(8,128)} copy(f32[48,8,128]{2,1,0:T(8,128)S(1)} %get-tuple-element.10) | data formatting | bytes 393216
  60.7 0.7 %copy.15 = f32[48,8,128]{2,1,0:T(8,128)} copy(f32[48,8,128]{2,1,0:T(8,128)S(1)} %get-tuple-element.11) | data formatting | bytes 393216
  61.4 0.7 %copy.16 = f32[48,8,128]{2,1,0:T(8,128)} copy(f32[48,8,128]{2,1,0:T(8,128)S(1)} %get-tuple-element.12) | data formatting | bytes 393216
  62.0 0.6 copy.17
  62.6 0.6 copy.18
Async XLA Ops:
  0.6 0.9 %copy-start = (f32[48,8,128]{2,1,0:T(8,128)S(1)}, f32[48,8,128]{2,1,0:T(8,128)}, u32[]{:S(2)}) copy-start(f32[48,8,128]{2,1,0:T(8,128)} %refs_0_.1) | copy-start | bytes 589828
  1.6 0.9 %copy-start.1 = (f32[48,8,128]{2,1,0:T(8,128)S(1)}, f32[48,8,128]{2,1,0:T(8,128)}, u32[]{:S(2)}) copy-start(f32[48,8,128]{2,1,0:T(8,128)} %refs_1_.1) | copy-start | bytes 589828
  2.5 0.9 %copy-start.2 = (f32[48,8,128]{2,1,0:T(8,128)S(1)}, f32[48,8,128]{2,1,0:T(8,128)}, u32[]{:S(2)}) copy-start(f32[48,8,128]{2,1,0:T(8,128)} %refs_2_.1) | copy-start | bytes 589828
  3.4 0.7 %copy-start.3 = (s32[8,128]{1,0:T(8,128)S(1)}, s32[8,128]{1,0:T(8,128)}, u32[]{:S(2)}) copy-start(s32[8,128]{1,0:T(8,128)} %refs_3_.1) | copy-start | bytes 12292

commit v2 on v1

--- a/solution.py
+++ b/solution.py
@@ -67,15 +67,16 @@
     nby, nbx,
     temp_in, uvel_in, vvel_in, kmt_in,
     temp_out, uvel_out, vvel_out, surface_out, resid_out,
-    raw, kmt_v, pad_t, pad_u, pad_v, star_t, star_u, star_v, fresh, surf_v, resid_v, depth_v, depths_v, q_ref, qs_ref,
+    raw, kmt_v, pad_t, pad_u, pad_v, star_t, star_u, star_v, depth_v, depths_v, q_ref, qs_ref,
     tx_row1, tx_row2, tx_col, tx_cor, rx_row1, rx_row2, rx_col, rx_cor,
     tx_u, rx_u, tx_bx, rx_bx, tx_by, rx_by,
-    in_sem, out_sem, row1_s, row1_r, row2_s, row2_r, col_s, col_r, cor_s, cor_r, u_s, u_r, bx_s, bx_r, by_s, by_r,
+    in_sem, row1_s, row1_r, row2_s, row2_r, col_s, col_r, cor_s, cor_r, u_s, u_r, bx_s, bx_r, by_s, by_r,
     known,
 ):
     by, bx = lax.axis_index("by"), lax.axis_index("bx")
     pads = (pad_t, pad_u, pad_v)
     stars = (star_t, star_u, star_v)
+    fresh = (temp_out, uvel_out, vvel_out)
 
     def device(dy, dx):
         return (lax.rem(by + dy + nby, nby), lax.rem(bx + dx + nbx, nbx))
@@ -327,7 +328,7 @@
                     below = view[pl.ds(base - PITCH, 8), :]
                     value = own * cell + F32(STEP_SMOOTH) * ((e + w) + (n + s)) + F32(STEP_VERT) * (above + below)
                     value = jnp.where(centre, value, F32(0.0))
-                    fresh[f, c * CHUNK + l] = value
+                    fresh[f][c * CHUNK + l] = value
                     if f == 0:
                         total = total + value
             return total
@@ -354,10 +355,6 @@
     ]
     for copy in round_u:
         copy.start()
-    saves = [
-        pltpu.make_async_copy(fresh.at[f], dst, out_sem.at[f]) for f, dst in enumerate((temp_out, uvel_out, vvel_out))
-    ]
-    saves[0].start()
     for copy in round_u:
         copy.wait_recv()
     pl.semaphore_wait(known.at[1], 2)
@@ -402,8 +399,6 @@
     star_cols([1, 2])
     star_own([1, 2])
     update_own([1, 2])
-    saves[1].start()
-    saves[2].start()
     for copy in first + row2 + round_u:
         copy.wait_send()
     remote(rx_bx, rx_bx, bx_s, bx_r, east).wait_send()
@@ -443,15 +438,18 @@
     resid = z[0] * weighted[0]
     for i in range(1, ITERS + 1):
         resid = resid + z[i] * weighted[i]
-    surf_v[...] = surface
-    resid_v[...] = resid
-    saves.append(pltpu.make_async_copy(surf_v, surface_out, out_sem.at[3]))
-    saves.append(pltpu.make_async_copy(resid_v, resid_out, out_sem.at[4]))
-    saves[3].start()
-    saves[4].start()
+    surface_out[...] = surface
+    resid_out[...] = resid
     remote(rx_by, rx_by, by_s, by_r, north).wait_send()
-    for save in saves:
-        save.wait()
+
+
+def store(*refs):
+    sources, targets, sems = refs[:5], refs[5:10], refs[10]
+    copies = [pltpu.make_async_copy(src, dst, sems.at[i]) for i, (src, dst) in enumerate(zip(sources, targets))]
+    for copy in copies:
+        copy.start()
+    for copy in copies:
+        copy.wait()
 
 
 def solution(mesh):
@@ -461,18 +459,15 @@
         field = jax.ShapeDtypeStruct(temp.shape, F32)
         plane = jax.ShapeDtypeStruct(kmt.shape, F32)
         vmem, dma = pltpu.VMEM, pltpu.SemaphoreType.DMA
-        return pl.pallas_call(
+        results = pl.pallas_call(
             lambda *refs: kernel(nby, nbx, *refs),
-            out_shape=(field, field, field, plane, plane),
-            in_specs=[pl.BlockSpec(memory_space=pl.ANY)] * 4,
-            out_specs=(pl.BlockSpec(memory_space=pl.ANY),) * 5,
+            out_shape=(*[pltpu.VMEM(temp.shape, F32)] * 3, *[pltpu.VMEM(kmt.shape, F32)] * 2),
+            in_specs=[pl.BlockSpec(memory_space=pltpu.HBM)] * 4,
+            out_specs=(pl.BlockSpec(memory_space=pltpu.VMEM),) * 5,
             scratch_shapes=[
                 vmem((3, KL, ROWS, COLS), F32),
                 vmem((ROWS, COLS), jnp.int32),
                 *[vmem((PADDED, COLS), F32)] * 6,
-                vmem((3, KL, ROWS, COLS), F32),
-                vmem((ROWS, COLS), F32),
-                vmem((ROWS, COLS), F32),
                 vmem((ROWS, COLS), F32),
                 vmem((5, 2 * ROWS, 2 * COLS), F32),
                 vmem((6, ROWS, COLS), F32),
@@ -491,7 +486,7 @@
                 vmem((nbx - 1, 1, COLS), F32),
                 vmem((1, COLS), F32),
                 vmem((nby - 1, 1, COLS), F32),
-                dma((4,)), dma((5,)),
+                dma((4,)),
                 dma((2,)), dma((2,)), dma((2,)), dma((2,)),
                 dma((2,)), dma((2,)), dma((4,)), dma((4,)),
                 dma((8,)), dma((8,)),
@@ -501,7 +496,15 @@
             compiler_params=pltpu.CompilerParams(
                 collective_id=0, has_side_effects=True, vmem_limit_bytes=32 * 1024 * 1024
             ),
-        )(temp, uvel, vvel, kmt)
+        )(*[pltpu.with_memory_space_constraint(a, pltpu.HBM) for a in (temp, uvel, vvel, kmt)])
+        return pl.pallas_call(
+            store,
+            out_shape=(field, field, field, plane, plane),
+            in_specs=[pl.BlockSpec(memory_space=pltpu.VMEM)] * 5,
+            out_specs=(pl.BlockSpec(memory_space=pltpu.HBM),) * 5,
+            scratch_shapes=[dma((5,))],
+            name="store",
+        )(*[pltpu.with_memory_space_constraint(r, pltpu.VMEM) for r in results])
 
     in_specs = (P(None, "by", "bx"), P(None, "by", "bx"), P(None, "by", "bx"), P("by", "bx"))
     out_specs = (

time: 63.5 us -> 56.6 us (0.89)
  local copies, waits for them, and re-layouts: 6.68 us -> 0 us
    unnamed x13 -> x0, local copies, waits for them, and re-layouts: 6.68 us -> none
    pallas_call x1 -> x2, Pallas kernels: 55.9 us -> 55.8 us  [the longest x1 54.9 us: on_device(): pl.pallas_call(lambda *refs: kernel(nby, nbx, *refs), out_shape=(*[pltpu....]
where the time goes in v2:
time: 56.6 us; the launch traced here: 56.4 us
  Pallas kernels  55.8 us (99%)
  between operations  0.64 us (1%)
    pallas_call x1, Pallas kernels, on_device(): pl.pallas_call(lambda *refs: kernel(nby, nbx, *refs), out_shape=(*[pltpu....  54.9 us

profile of v2, /device:TPU:1, one launch (start us, length us, event | category | flops | bytes accessed | tf_op | source)
XLA Modules:
  0.0 56.4 jit_solution(11248844848792959423)
XLA Ops:
  0.6 54.9 %shard_map.83 = (f32[48,8,128]{2,1,0:T(8,128)S(1)}, f32[48,8,128]{2,1,0:T(8,128)S(1)}, f32[48,8,128]{2,1,0:T(8,128)S(1)}, f32[8,128]{1,0:T(8,128)S(1)}, f32[8,128]{1,0:T(8,128)S(1)}) custom-call(f32[48,8,128]{2,1,0:T(8,128)} %refs_0_.1, f32[48,8,128]{2,1,0:T(8,128)} %refs_1_.1, f32[48,8,128]{2,1,0:T(8,128)} %refs_2_.1, s32[8,128]{1,0:T(8,128)} %refs_3_.1), custom_call_target="tpu_custom_call" | custom-call | tf_op jit(solution)/shard_map/pallas_call | solution.py:462
  55.6 0.9 %store.1 = (f32[48,8,128]{2,1,0:T(8,128)}, f32[48,8,128]{2,1,0:T(8,128)}, f32[48,8,128]{2,1,0:T(8,128)}, f32[8,128]{1,0:T(8,128)}, f32[8,128]{1,0:T(8,128)}) custom-call(f32[48,8,128]{2,1,0:T(8,128)S(1)} %get-tuple-element.10.refs_0_, f32[48,8,128]{2,1,0:T(8,128)S(1)} %get-tuple-element.11.refs_1_, f32[48,8,128]{2,1,0:T(8,128)S(1)} %get-tuple-element.12.refs_2_, ...), custom_call_target="tpu_custom_call" | custom-call | tf_op jit(solution)/shard_map/store/pallas_call | solution.py:500

commit v3 on v2

--- a/solution.py
+++ b/solution.py
@@ -19,6 +19,7 @@
 PITCH = 16
 PADDED = PITCH * (KL + 2)
 RADIUS = 4
+WIDTH = 4
 
 F32 = jnp.float32
 MESH = pl.DeviceIdType.MESH
@@ -61,6 +62,71 @@
     for factor, side in zip(factors, sides):
         total = total + factor * side
     return jnp.where(centre, total, F32(0.0))
+
+
+def two_sum(a, b):
+    head = a + b
+    shift = head - a
+    return head, (a - (head - shift)) + (b - shift)
+
+
+def quick_sum(a, b):
+    head = a + b
+    return head, b - (head - a)
+
+
+def halves(a):
+    wide = a * F32(4097.0)
+    head = wide - (wide - a)
+    return head, a - head
+
+
+def two_prod(a, b):
+    head = a * b
+    (ah, al), (bh, bl) = halves(a), halves(b)
+    return head, ((ah * bh - head) + ah * bl + al * bh) + al * bl
+
+
+def add2(a, b):
+    head, tail = two_sum(a[0], b[0])
+    return quick_sum(head, tail + (a[1] + b[1]))
+
+
+def sub2(a, b):
+    return add2(a, (-b[0], -b[1]))
+
+
+def minor(a, b, c, d):
+    one, one_tail = two_prod(a[0], b[0])
+    two, two_tail = two_prod(c[0], d[0])
+    value, lost = two_sum(one, -two)
+    one_tail = one_tail + (a[0] * b[1] + a[1] * b[0])
+    return value + (lost + (one_tail - (two_tail + (c[0] * d[1] + c[1] * d[0]))))
+
+
+def sum_rows(tiles):
+    sub = lax.broadcasted_iota(jnp.int32, (8, COLS), 0)
+    for shift in (1, 2, 4):
+        mine = sub % (2 * shift) < shift
+        tiles = [
+            jnp.where(mine, one, other) + roll(jnp.where(mine, other, one), shift, 0)
+            for one, other in zip(tiles[0::2], tiles[1::2])
+        ]
+    return tiles
+
+
+def add_exact(rows):
+    terms = [(row, None) for row in rows]
+    while len(terms) > 1:
+        paired = []
+        for (a, lost_a), (b, lost_b) in zip(terms[0::2], terms[1::2]):
+            head, lost = two_sum(a, b)
+            for more in (lost_a, lost_b):
+                lost = lost if more is None else lost + more
+            paired.append((head, lost))
+        terms = paired + ([terms[-1]] if len(terms) % 2 else [])
+    total, lost = terms[0]
+    return total, jnp.zeros_like(total) if lost is None else lost
 
 
 def kernel(
@@ -91,9 +157,17 @@
         load.start()
 
     barrier = pltpu.get_barrier_semaphore()
-    greeted = [device(0, o) for o in range(1, nbx)]
+    across = lax.rem(bx, WIDTH)
+    line = bx - across
+    plane = [
+        (by, line + lax.rem(across + 1, WIDTH)),
+        (by, line + lax.rem(across + WIDTH - 1, WIDTH)),
+        device(0, WIDTH),
+        device(0, -WIDTH),
+    ]
+    greeted = [device(dy, dx) for dy, dx in DIRS if dx]
     greeted += [device(d, 0) for d in range(-RADIUS, RADIUS + 1) if d]
-    greeted += [device(dy, dx) for dy, dx in DIRS if dy and dx]
+    greeted += plane
     for dev in greeted:
         pl.semaphore_signal(barrier, inc=1, device_id=dev, device_id_type=MESH)
 
@@ -108,23 +182,17 @@
         loads[1 + f].wait()
         pad = pads[f]
 
-        def pack(c, carry, f=f, pad=pad):
+        quads = []
+        for c in range(KL // CHUNK):
             packed = jnp.zeros((8, COLS), F32)
-            rows = pad.at[pl.ds(pl.multiple_of(c * (PITCH * CHUNK), PITCH * CHUNK), PITCH * (CHUNK + 2)), :]
             for l in range(CHUNK):
-                tile = raw[f, c * CHUNK + l]
-                rows[pl.ds(PITCH * (l + 1), 8), :] = tile
-                packed = jnp.where(lane8 // 4 == l, roll(tile, 2 + 4 * l, 1), packed)
-            quarter = lax.rem(c, 4)
-            packed = roll(packed, 32 * quarter, 1)
-            half = c // 4
-            before = tx_col[2 * f + half]
-            tx_col[2 * f + half] = jnp.where(lane8 // 32 == quarter, packed, before)
-            return carry
-
-        for half in range(2):
-            tx_col[2 * f + half] = jnp.zeros((8, COLS), F32)
-        lax.fori_loop(0, KL // CHUNK, pack, 0)
+                k = c * CHUNK + l
+                tile = raw[f, k]
+                pad[PITCH * (k + 1) : PITCH * (k + 1) + 8, :] = tile
+                packed = jnp.where(lane8 // 4 == k % 32, roll(tile, 2 + 4 * (k % 32), 1), packed)
+            quads.append(packed)
+        tx_col[2 * f] = (quads[0] + quads[1]) + (quads[2] + quads[3])
+        tx_col[2 * f + 1] = quads[4] + quads[5]
     tx_col[6] = depth_v[...]
 
     def edge_row(f, row):
@@ -182,20 +250,29 @@
     for copy in first + row2:
         copy.start()
 
-    def tell(step, reach):
-        for d in (-reach, reach):
+    def tell(step):
+        for d in (-(RADIUS << step), RADIUS << step):
             pl.semaphore_signal(known.at[step], inc=1, device_id=device(d, 0), device_id_type=MESH)
-
-    tell(0, RADIUS)
+        for dev in plane:
+            pl.semaphore_signal(known.at[3 + step], inc=1, device_id=dev, device_id_type=MESH)
+
+    def told_by(step):
+        pl.semaphore_wait(known.at[step], 2)
+
+    def told_bx(step):
+        pl.semaphore_wait(known.at[3 + step], len(plane))
+
+    tell(0)
 
     for star in stars:
         star[0:PITCH, :] = jnp.zeros((PITCH, COLS), F32)
         star[PADDED - PITCH : PADDED, :] = jnp.zeros((PITCH, COLS), F32)
 
+    told_by(0)
+    told_bx(0)
+    tell(1)
     for copy in first:
         copy.wait_recv()
-    pl.semaphore_wait(known.at[0], 2)
-    tell(1, 2 * RADIUS)
 
     dep = {
         S: keep_s * rx_row1[0, 4 * KL : 4 * KL + 8],
@@ -285,7 +362,7 @@
         shift = lax.rem(2 * COLS - 2 - 32 * lax.rem(c, 4) - 4 * l, COLS)
         return roll(ref[2 * f + c // 4], shift, 1)
 
-    def star_own(fields):
+    def star_own(fields, unroll):
         def step(c, carry):
             near = near_own()
             views = [chunk_rows(pad, c) for pad in pads]
@@ -304,9 +381,9 @@
                     outs[f][pl.ds(base, 8), :] = star_value(terms, cell, (e, w, n, s))
             return carry
 
-        lax.fori_loop(0, KL // CHUNK, step, 0)
-
-    def update_own(fields):
+        lax.fori_loop(0, KL // CHUNK, step, 0, unroll=unroll)
+
+    def update_own(fields, unroll):
         def step(c, total):
             near = near_own()
             views = [chunk_rows(star, c) for star in stars]
@@ -333,12 +410,12 @@
                         total = total + value
             return total
 
-        return lax.fori_loop(0, KL // CHUNK, step, jnp.zeros((8, COLS), F32))
+        return lax.fori_loop(0, KL // CHUNK, step, jnp.zeros((8, COLS), F32), unroll=unroll)
 
     star_rows([0], lambda side, f: (keep_s, keep_n)[side] * rx_row1[side, KL : 2 * KL])
     star_cols([0])
-    star_own([0])
-    rhs = update_own([0]) * F32(1.0 / math.sqrt(KL))
+    star_own([0], True)
+    rhs = update_own([0], True) * F32(1.0 / math.sqrt(KL))
 
     height = depths_v[0] * F32(1.0 / KL)
     w_e = jnp.minimum(height, roll(height, -1, 1))
@@ -355,12 +432,14 @@
     ]
     for copy in round_u:
         copy.start()
+    told_by(1)
+    told_bx(1)
+    tell(2)
     for copy in round_u:
         copy.wait_recv()
-    pl.semaphore_wait(known.at[1], 2)
-    tell(2, 4 * RADIUS)
 
     power = patch(tx_u[...], {d: rx_u[d] for d in range(8)})
+    largest = jnp.max(jnp.max(jnp.abs(power), axis=0, keepdims=True), axis=1, keepdims=True)
     powers = [power]
     for _ in range(ITERS):
         e, w = roll(power, -1, 1), roll(power, 1, 1)
@@ -369,27 +448,46 @@
         powers.append(power)
     own_diag = diag[0:8, 0:COLS]
     powers = [p[0:8, 0:COLS] for p in powers]
-    weighted = [own_diag * p for p in powers]
-
-    row = jnp.zeros((1, COLS), F32)
+    steps = [powers[i] - powers[i + 1] for i in range(ITERS)]
+
+    count = len(GRAM)
+    grid = F32(4096.0 * 4.5) * largest * largest
+    finer = grid * F32(1.0 / 4096.0)
+    levels = ([], [], [])
+    for i, j in GRAM:
+        head, tail = two_prod(powers[i], powers[j])
+        wide, extra = two_prod(own_diag, head)
+        extra = extra + own_diag * tail
+        coarse = (wide + grid) - grid
+        wide = wide - coarse
+        fine = (wide + finer) - finer
+        for held, part in zip(levels, (coarse, fine, (wide - fine) + extra)):
+            held.append(part)
+    tiles = levels[0] + levels[1] + levels[2]
+    tiles += [jnp.zeros((8, COLS), F32)] * (-len(tiles) % 8)
+    row = jnp.zeros((8, COLS), F32)
+    for c, tile in enumerate(sum_rows(tiles)):
+        row = row + jnp.where(lane8 == sub8 + 8 * c, jnp.sum(tile, axis=1, keepdims=True), F32(0.0))
+    row = jnp.sum(row, axis=0, keepdims=True)
     lane1 = lanes_of((1, COLS))
-    for k, (i, j) in enumerate(GRAM):
-        part = jnp.sum(jnp.sum(weighted[i] * powers[j], axis=0, keepdims=True), axis=1, keepdims=True)
-        row = jnp.where(lane1 == k, part, row)
+    last = jnp.logical_and(lane1 >= 2 * count, lane1 < 3 * count)
 
     tx_bx[...] = row
+    told_bx(2)
     over_bx = [
         remote(tx_bx, rx_bx.at[o - 1], bx_s, bx_r, device(0, o)) for o in range(1, nbx)
     ]
     for copy in over_bx:
         copy.start()
     remote(rx_bx, rx_bx, bx_s, bx_r, east).wait_recv()
-    row = row + jnp.sum(rx_bx[...], axis=0)
-    pl.semaphore_wait(known.at[2], 2)
-
+    row, lost = add_exact([row] + [rx_bx[i] for i in range(nbx - 1)])
+    row = row + jnp.where(last, roll(lost, 2 * count, 1) + roll(lost, count, 1), F32(0.0))
+
+    told_by(2)
     tx_by[...] = row
+    rx_by[0:1, :] = row
     order = sorted(range(1, nby), key=lambda o: -min(o, nby - o))
-    over_by = [remote(tx_by, rx_by.at[o - 1], by_s, by_r, device(o, 0)) for o in order]
+    over_by = [remote(tx_by, rx_by.at[pl.ds(o, 1), :], by_s, by_r, device(o, 0)) for o in order]
     for copy in over_by:
         copy.start()
 
@@ -397,50 +495,49 @@
         copy.wait_recv()
     star_rows([1, 2], lambda side, f: (keep_s, keep_n)[side] * rx_row2[side, (f - 1) * KL : f * KL])
     star_cols([1, 2])
-    star_own([1, 2])
-    update_own([1, 2])
+    star_own([1, 2], 1)
+    update_own([1, 2], 1)
     for copy in first + row2 + round_u:
         copy.wait_send()
     remote(rx_bx, rx_bx, bx_s, bx_r, east).wait_send()
 
-    remote(rx_by, rx_by, by_s, by_r, north).wait_recv()
-    row = row + jnp.sum(rx_by[...], axis=0)
+    others = rx_by.at[pl.ds(1, nby - 1), :]
+    remote(others, others, by_s, by_r, north).wait_recv()
+    row, lost = add_exact([rx_by[i : i + 8] for i in range(0, nby, 8)])
+    for shift in (4, 2, 1):
+        row, more = two_sum(row, roll(row, shift, 0))
+        lost = (lost + roll(lost, shift, 0)) + more
+    row, lost = row[0:1], lost[0:1]
+    head, tail = two_sum(row, roll(row, -count, 1))
+    total = quick_sum(head, tail + ((roll(row, -2 * count, 1) + lost) + roll(lost, -count, 1)))
 
     gram = {}
     for k, (i, j) in enumerate(GRAM):
-        gram[i, j] = gram[j, i] = row[0:1, k : k + 1]
-
-    def inner(a, b):
-        total = None
-        for i, ai in enumerate(a):
-            for j, bj in enumerate(b):
-                term = ai * bj * gram[i, j]
-                total = term if total is None else total + term
-        return total
-
-    one = jnp.ones((1, 1), F32)
-    z, p, x = [one], [one], []
-    rz = inner(z, z)
-    for step in range(ITERS):
-        q = [p[0]] + [p[i] - p[i - 1] for i in range(1, len(p))] + [-p[-1]]
-        alpha = rz / inner(p, q)
-        x = [x[i] + alpha * p[i] if i < len(x) else alpha * p[i] for i in range(len(p))]
-        z = [z[i] - alpha * q[i] if i < len(z) else -(alpha * q[i]) for i in range(len(q))]
-        if step + 1 < ITERS:
-            rz_next = inner(z, z)
-            beta = rz_next / rz
-            p = [z[i] + beta * p[i] if i < len(p) else z[i] for i in range(len(z))]
-            rz = rz_next
-
-    surface = x[0] * powers[0]
-    for i in range(1, ITERS):
-        surface = surface + x[i] * powers[i]
-    resid = z[0] * weighted[0]
-    for i in range(1, ITERS + 1):
-        resid = resid + z[i] * weighted[i]
+        gram[i, j] = gram[j, i] = tuple(part[0:1, k : k + 1] for part in total)
+    system = [[sub2(gram[i, j], gram[i, j + 1]) for j in range(ITERS)] + [gram[i, 0]] for i in range(ITERS)]
+    top = system[0]
+    over = F32(1.0) / top[0][0]
+    lower = []
+    for i in (1, 2):
+        ratio = system[i][0][0] * over
+        left = []
+        for j in range(ITERS + 1):
+            head, tail = two_prod(ratio, top[j][0])
+            value, lost = two_sum(system[i][j][0], -head)
+            left.append((value, lost + (system[i][j][1] - (tail + ratio * top[j][1]))))
+        ratio = (left[0][0] + left[0][1]) * over
+        lower.append([quick_sum(left[j][0], left[j][1] - ratio * top[j][0]) for j in range(1, ITERS + 1)])
+    (a11, a12, b1), (a21, a22, b2) = lower
+    det = F32(1.0) / minor(a11, a22, a12, a21)
+    c1 = minor(b1, a22, b2, a12) * det
+    c2 = minor(b2, a11, b1, a21) * det
+    c0 = ((top[3][0] - top[1][0] * c1) - top[2][0] * c2) * over
+
+    surface = (c0 * powers[0] + c1 * powers[1]) + c2 * powers[2]
+    resid = own_diag * (((powers[0] - c0 * steps[0]) - c1 * steps[1]) - c2 * steps[2])
     surface_out[...] = surface
     resid_out[...] = resid
-    remote(rx_by, rx_by, by_s, by_r, north).wait_send()
+    remote(others, others, by_s, by_r, north).wait_send()
 
 
 def store(*refs):
@@ -485,13 +582,13 @@
                 vmem((1, COLS), F32),
                 vmem((nbx - 1, 1, COLS), F32),
                 vmem((1, COLS), F32),
-                vmem((nby - 1, 1, COLS), F32),
+                vmem((nby, COLS), F32),
                 dma((4,)),
                 dma((2,)), dma((2,)), dma((2,)), dma((2,)),
                 dma((2,)), dma((2,)), dma((4,)), dma((4,)),
                 dma((8,)), dma((8,)),
                 dma, dma, dma, dma,
-                pltpu.SemaphoreType.REGULAR((3,)),
+                pltpu.SemaphoreType.REGULAR((6,)),
             ],
             compiler_params=pltpu.CompilerParams(
                 collective_id=0, has_side_effects=True, vmem_limit_bytes=32 * 1024 * 1024

time: 56.6 us -> 56.5 us (level)
  no operation moved by 1% of the time
where the time goes in v3:
time: 56.5 us; the launch traced here: 56.3 us
  Pallas kernels  55.7 us (99%)
  between operations  0.64 us (1%)
    pallas_call x1, Pallas kernels, on_device(): pl.pallas_call(lambda *refs: kernel(nby, nbx, *refs), out_shape=(*[pltpu....  54.9 us

profile of v3, /device:TPU:1, one launch (start us, length us, event | category | flops | bytes accessed | tf_op | source)
XLA Modules:
  0.0 56.3 jit_solution(3154161804957933920)
XLA Ops:
  0.6 54.9 %shard_map.83 = (f32[48,8,128]{2,1,0:T(8,128)S(1)}, f32[48,8,128]{2,1,0:T(8,128)S(1)}, f32[48,8,128]{2,1,0:T(8,128)S(1)}, f32[8,128]{1,0:T(8,128)S(1)}, f32[8,128]{1,0:T(8,128)S(1)}) custom-call(f32[48,8,128]{2,1,0:T(8,128)} %refs_0_.1, f32[48,8,128]{2,1,0:T(8,128)} %refs_1_.1, f32[48,8,128]{2,1,0:T(8,128)} %refs_2_.1, s32[8,128]{1,0:T(8,128)} %refs_3_.1), custom_call_target="tpu_custom_call" | custom-call | tf_op jit(solution)/shard_map/pallas_call | solution.py:559
  55.5 0.9 %store.1 = (f32[48,8,128]{2,1,0:T(8,128)}, f32[48,8,128]{2,1,0:T(8,128)}, f32[48,8,128]{2,1,0:T(8,128)}, f32[8,128]{1,0:T(8,128)}, f32[8,128]{1,0:T(8,128)}) custom-call(f32[48,8,128]{2,1,0:T(8,128)S(1)} %get-tuple-element.10.refs_0_, f32[48,8,128]{2,1,0:T(8,128)S(1)} %get-tuple-element.11.refs_1_, f32[48,8,128]{2,1,0:T(8,128)S(1)} %get-tuple-element.12.refs_2_, ...), custom_call_target="tpu_custom_call" | custom-call | tf_op jit(solution)/shard_map/store/pallas_call | solution.py:597

commit v4 on v3

--- a/solution.py
+++ b/solution.py
@@ -133,7 +133,7 @@
     nby, nbx,
     temp_in, uvel_in, vvel_in, kmt_in,
     temp_out, uvel_out, vvel_out, surface_out, resid_out,
-    raw, kmt_v, pad_t, pad_u, pad_v, star_t, star_u, star_v, depth_v, depths_v, q_ref, qs_ref,
+    raw, kmt_v, pad_t, pad_u, pad_v, star_t, star_u, star_v, depth_v, depths_v, q_ref, qs_ref, own_ref, beyond_ref,
     tx_row1, tx_row2, tx_col, tx_cor, rx_row1, rx_row2, rx_col, rx_cor,
     tx_u, rx_u, tx_bx, rx_bx, tx_by, rx_by,
     in_sem, row1_s, row1_r, row2_s, row2_r, col_s, col_r, cor_s, cor_r, u_s, u_r, bx_s, bx_r, by_s, by_r,
@@ -268,6 +268,38 @@
         star[0:PITCH, :] = jnp.zeros((PITCH, COLS), F32)
         star[PADDED - PITCH : PADDED, :] = jnp.zeros((PITCH, COLS), F32)
 
+    def chunk_rows(ref, c):
+        return ref.at[pl.ds(pl.multiple_of(c * (PITCH * CHUNK), PITCH * CHUNK), PITCH * (CHUNK + 2)), :]
+
+    inside = [
+        depth_v[...],
+        jnp.where(lane8 == COLS - 1, F32(0.0), roll(depth_v[...], -1, 1)),
+        jnp.where(lane8 == 0, F32(0.0), roll(depth_v[...], 1, 1)),
+        jnp.where(sub8 == ROWS - 1, F32(0.0), roll(depth_v[...], -1, 0)),
+        jnp.where(sub8 == 0, F32(0.0), roll(depth_v[...], 1, 0)),
+    ]
+
+    def star_inside(c, carry):
+        views = [chunk_rows(pad, c) for pad in pads]
+        out = chunk_rows(star_t, c)
+        for l in range(CHUNK):
+            base = PITCH * (l + 1)
+            level = (c * CHUNK + l).astype(F32)
+            terms = star_terms(level, inside, views[1][pl.ds(base, 8), :], views[2][pl.ds(base, 8), :])
+            cell = views[0][pl.ds(base, 8), :]
+            e = jnp.where(lane8 == COLS - 1, F32(0.0), roll(cell, -1, 1))
+            w = jnp.where(lane8 == 0, F32(0.0), roll(cell, 1, 1))
+            n = jnp.where(sub8 == ROWS - 1, F32(0.0), roll(cell, -1, 0))
+            s = jnp.where(sub8 == 0, F32(0.0), roll(cell, 1, 0))
+            out[pl.ds(base, 8), :] = star_value(terms, cell, (e, w, n, s))
+            smooth = [jnp.where(level < d, F32(STEP_SMOOTH), F32(0.0)) for d in inside[1:]]
+            up = jnp.where(level + F32(1.0) < inside[0], F32(STEP_VERT), F32(0.0))
+            down = jnp.where(level > F32(0.0), F32(STEP_VERT), F32(0.0))
+            own_ref[c * CHUNK + l] = F32(1.0) - (((smooth[0] + smooth[1]) + (smooth[2] + smooth[3])) + (up + down))
+        return carry
+
+    lax.fori_loop(0, KL // CHUNK, star_inside, 0)
+
     told_by(0)
     told_bx(0)
     tell(1)
@@ -354,9 +386,6 @@
 
     def near_own():
         return [depths_v[i, 0:8, 0:COLS] for i in range(5)]
-
-    def chunk_rows(ref, c):
-        return ref.at[pl.ds(pl.multiple_of(c * (PITCH * CHUNK), PITCH * CHUNK), PITCH * (CHUNK + 2)), :]
 
     def edge_of(ref, f, c, l):
         shift = lax.rem(2 * COLS - 2 - 32 * lax.rem(c, 4) - 4 * l, COLS)
@@ -412,10 +441,58 @@
 
         return lax.fori_loop(0, KL // CHUNK, step, jnp.zeros((8, COLS), F32), unroll=unroll)
 
+    def add_beyond():
+        for side, row in enumerate((0, ROWS - 1)):
+            cell, halo = edge_row(0, row), rows1[side, 0]
+            adv = F32(0.5 * STEP_ADV) * edge_row(2, row)
+            centre = level_rows < depths_v[0, row : row + 1, 0:COLS]
+            beyond = level_rows < depths_v[4 - side, row : row + 1, 0:COLS]
+            more = jnp.where(beyond, F32(STEP_DIFF) * (halo - cell), F32(0.0))
+            more = more + adv * halo if side == 0 else more - adv * halo
+            place = pl.ds(PITCH + row, KL, stride=PITCH)
+            star_t[place, :] = star_t[place, :] + jnp.where(centre, more, F32(0.0))
+        here = jnp.where(odd, depth_v[:, 0:1], depth_v[:, COLS - 1 : COLS])
+        near = jnp.where(odd, depths_v[0, 0:8, 2 * COLS - 1 : 2 * COLS], depths_v[0, 0:8, COLS : COLS + 1])
+        for half in range(2):
+            level = (lane8 // 4 + 32 * half).astype(F32)
+            cell = tx_col[half]
+            halo = jnp.where(odd, roll(q_ref[half], 1, 1), roll(q_ref[half], -1, 1))
+            adv = F32(0.5 * STEP_ADV) * tx_col[2 + half] * halo
+            more = jnp.where(level < near, F32(STEP_DIFF) * (halo - cell), F32(0.0)) + jnp.where(odd, adv, -adv)
+            beyond_ref[half] = jnp.where(level < here, more, F32(0.0))
+        rim = jnp.logical_or(lane8 == 0, lane8 == COLS - 1)
+        for k in range(KL):
+            place = pl.ds(PITCH * (k + 1), 8)
+            edge = roll(beyond_ref[k // 32], COLS - 2 - 4 * (k % 32), 1)
+            star_t[place, :] = star_t[place, :] + jnp.where(rim, edge, F32(0.0))
+
+    def update_tracer():
+        rim_rows = jnp.where(sub8 == 0, depths_v[4, 0:8, 0:COLS], F32(0.0))
+        rim_rows = jnp.where(sub8 == ROWS - 1, depths_v[3, 0:8, 0:COLS], rim_rows)
+        rim_lanes = jnp.where(lane8 == 0, depths_v[2, 0:8, 0:COLS], F32(0.0))
+        rim_lanes = jnp.where(lane8 == COLS - 1, depths_v[1, 0:8, 0:COLS], rim_lanes)
+        depth_own = depth_v[...]
+        total = [jnp.zeros((8, COLS), F32)] * 4
+        for k in range(KL):
+            base = PITCH * (k + 1)
+            cell = star_t[pl.ds(base, 8), :]
+            e, w = east_west(cell, roll(qs_ref[k // 32], COLS - 2 - 4 * (k % 32), 1))
+            n = star_t[pl.ds(base + 1, 8), :]
+            s = star_t[pl.ds(base - 1, 8), :]
+            above = star_t[pl.ds(base + PITCH, 8), :]
+            below = star_t[pl.ds(base - PITCH, 8), :]
+            own = own_ref[k] - jnp.where(rim_rows > F32(k), F32(STEP_SMOOTH), F32(0.0))
+            own = own - jnp.where(rim_lanes > F32(k), F32(STEP_SMOOTH), F32(0.0))
+            value = own * cell + F32(STEP_SMOOTH) * ((e + w) + (n + s)) + F32(STEP_VERT) * (above + below)
+            value = jnp.where(depth_own > F32(k), value, F32(0.0))
+            temp_out[k] = value
+            total[k % 4] = total[k % 4] + value
+        return (total[0] + total[1]) + (total[2] + total[3])
+
+    add_beyond()
     star_rows([0], lambda side, f: (keep_s, keep_n)[side] * rx_row1[side, KL : 2 * KL])
     star_cols([0])
-    star_own([0], True)
-    rhs = update_own([0], True) * F32(1.0 / math.sqrt(KL))
+    rhs = update_tracer() * F32(1.0 / math.sqrt(KL))
 
     height = depths_v[0] * F32(1.0 / KL)
     w_e = jnp.minimum(height, roll(height, -1, 1))
@@ -569,6 +646,8 @@
                 vmem((5, 2 * ROWS, 2 * COLS), F32),
                 vmem((6, ROWS, COLS), F32),
                 vmem((6, ROWS, COLS), F32),
+                vmem((KL, ROWS, COLS), F32),
+                vmem((2, ROWS, COLS), F32),
                 vmem((2, 4 * KL + 8, COLS), F32),
                 vmem((2, 2 * KL, COLS), F32),
                 vmem((7, ROWS, COLS), F32),

time: 56.5 us -> 53.9 us (0.954)
  Pallas kernels: 55.7 us -> 53.1 us
    pallas_call x1, Pallas kernels: 54.9 us -> 52.2 us  [on_device(): pl.pallas_call(lambda *refs: kernel(nby, nbx, *refs), out_shape=(*[pltpu....]
where the time goes in v4:
time: 53.9 us; the launch traced here: 53.7 us
  Pallas kernels  53.1 us (99%)
  between operations  0.64 us (1%)
    pallas_call x1, Pallas kernels, on_device(): pl.pallas_call(lambda *refs: kernel(nby, nbx, *refs), out_shape=(*[pltpu....  52.2 us

profile of v4, /device:TPU:1, one launch (start us, length us, event | category | flops | bytes accessed | tf_op | source)
XLA Modules:
  0.0 53.7 jit_solution(8898124817362340818)
XLA Ops:
  0.6 52.2 %shard_map.83 = (f32[48,8,128]{2,1,0:T(8,128)S(1)}, f32[48,8,128]{2,1,0:T(8,128)S(1)}, f32[48,8,128]{2,1,0:T(8,128)S(1)}, f32[8,128]{1,0:T(8,128)S(1)}, f32[8,128]{1,0:T(8,128)S(1)}) custom-call(f32[48,8,128]{2,1,0:T(8,128)} %refs_0_.1, f32[48,8,128]{2,1,0:T(8,128)} %refs_1_.1, f32[48,8,128]{2,1,0:T(8,128)} %refs_2_.1, s32[8,128]{1,0:T(8,128)} %refs_3_.1), custom_call_target="tpu_custom_call" | custom-call | tf_op jit(solution)/shard_map/pallas_call | solution.py:636
  52.8 0.9 %store.1 = (f32[48,8,128]{2,1,0:T(8,128)}, f32[48,8,128]{2,1,0:T(8,128)}, f32[48,8,128]{2,1,0:T(8,128)}, f32[8,128]{1,0:T(8,128)}, f32[8,128]{1,0:T(8,128)}) custom-call(f32[48,8,128]{2,1,0:T(8,128)S(1)} %get-tuple-element.10.refs_0_, f32[48,8,128]{2,1,0:T(8,128)S(1)} %get-tuple-element.11.refs_1_, f32[48,8,128]{2,1,0:T(8,128)S(1)} %get-tuple-element.12.refs_2_, ...), custom_call_target="tpu_custom_call" | custom-call | tf_op jit(solution)/shard_map/store/pallas_call | solution.py:676

commit v5 on v4

--- a/solution.py
+++ b/solution.py
@@ -590,7 +590,7 @@
 
     gram = {}
     for k, (i, j) in enumerate(GRAM):
-        gram[i, j] = gram[j, i] = tuple(part[0:1, k : k + 1] for part in total)
+        gram[i, j] = gram[j, i] = tuple(jnp.broadcast_to(part[0:1, k : k + 1], (8, COLS)) for part in total)
     system = [[sub2(gram[i, j], gram[i, j + 1]) for j in range(ITERS)] + [gram[i, 0]] for i in range(ITERS)]
     top = system[0]
     over = F32(1.0) / top[0][0]

time: 53.9 us -> 53.2 us (0.987)
  Pallas kernels: 53.1 us -> 52.3 us
    pallas_call x1, Pallas kernels: 52.2 us -> 51.5 us  [on_device(): pl.pallas_call(lambda *refs: kernel(nby, nbx, *refs), out_shape=(*[pltpu....]
where the time goes in v5:
time: 53.2 us; the launch traced here: 53 us
  Pallas kernels  52.3 us (98%)
  between operations  0.64 us (1%)
    pallas_call x1, Pallas kernels, on_device(): pl.pallas_call(lambda *refs: kernel(nby, nbx, *refs), out_shape=(*[pltpu....  51.5 us

profile of v5, /device:TPU:1, one launch (start us, length us, event | category | flops | bytes accessed | tf_op | source)
XLA Modules:
  0.0 53.0 jit_solution(15505289318530926162)
XLA Ops:
  0.6 51.5 %shard_map.83 = (f32[48,8,128]{2,1,0:T(8,128)S(1)}, f32[48,8,128]{2,1,0:T(8,128)S(1)}, f32[48,8,128]{2,1,0:T(8,128)S(1)}, f32[8,128]{1,0:T(8,128)S(1)}, f32[8,128]{1,0:T(8,128)S(1)}) custom-call(f32[48,8,128]{2,1,0:T(8,128)} %refs_0_.1, f32[48,8,128]{2,1,0:T(8,128)} %refs_1_.1, f32[48,8,128]{2,1,0:T(8,128)} %refs_2_.1, s32[8,128]{1,0:T(8,128)} %refs_3_.1), custom_call_target="tpu_custom_call" | custom-call | tf_op jit(solution)/shard_map/pallas_call | solution.py:636
  52.1 0.9 %store.1 = (f32[48,8,128]{2,1,0:T(8,128)}, f32[48,8,128]{2,1,0:T(8,128)}, f32[48,8,128]{2,1,0:T(8,128)}, f32[8,128]{1,0:T(8,128)}, f32[8,128]{1,0:T(8,128)}) custom-call(f32[48,8,128]{2,1,0:T(8,128)S(1)} %get-tuple-element.10.refs_0_, f32[48,8,128]{2,1,0:T(8,128)S(1)} %get-tuple-element.11.refs_1_, f32[48,8,128]{2,1,0:T(8,128)S(1)} %get-tuple-element.12.refs_2_, ...), custom_call_target="tpu_custom_call" | custom-call | tf_op jit(solution)/shard_map/store/pallas_call | solution.py:676
